TPU v7x, 32 devices: a whole 2x2x4 slice. The times are simulated.
32 devices in a mesh: groups: 2 (over y), space: 4 (over z), hidden: 2 (over x), sub: 2 (over core).
Axes of the slice: x: 2, y: 2, z: 4, core: 2. Of those that a mesh axis runs over, the one named last changes fastest.
Arguments:
- agent_state: bfloat16 [8192, 256], P(('groups', 'space')), parts along dimension 0, may hold values from -6 to 6
- members: int32 [8, 1024], P(('groups', 'space')), parts along dimension 0, may hold values from 0 to 1023, each once within a row
- norm_gain: float32 [256], replicated, may hold values from 0.1 to 1.9
- w_recv: bfloat16 [256, 1024], P(None, 'hidden'), may hold values from -0.375 to 0.375
- w_send: bfloat16 [256, 1024], P(None, 'hidden'), may hold values from -1.5 to 1.5
- w_out: bfloat16 [1024, 256], P('hidden'), may hold values from -0.1875 to 0.1875
- pair_list: int32 [512, 2], P(('groups', 'space', 'sub')), parts along dimension 0, may hold values from 0 to 31, as said below
- pair_counts: int32 [16], P(('groups', 'space', 'sub')), parts along dimension 0, may hold values from 0 to 32, as said below
- cotangent: bfloat16 [8192, 256], P(('groups', 'space')), parts along dimension 0, may hold values from -6 to 6
Outputs:
- new_state: bfloat16 [8192, 256], P(('groups', 'space', 'hidden', 'sub')), parts along dimension 0
- grad_state: float32 [8192, 256], P(('groups', 'space', 'hidden', 'sub')), parts along dimension 0
- grad_recv: float32 [512, 1024], P('groups', 'hidden'), parts along dimension 0
- grad_send: float32 [512, 1024], P('groups', 'hidden'), parts along dimension 0
- grad_out: float32 [2048, 256], P(('groups', 'hidden')), parts along dimension 0
There are 2 independent parts, one for each index of `groups`. A program takes and returns all parts, laid end to end along the dimension named above; an argument that names none is the same for every part. Nothing has to cross between parts.
Inputs may be any that keep to these rules, and one draw needn't show every extreme that they name: `pair_list`: rows p * 32 to p * 32 + pair_counts[p] - 1 hold the pairs of owning device p = 2 * (space index) + (sub index); each is (s, t) with s a block of that device's region and s < t <= s + 8; no pair appears twice in a part; other rows are 0. `pair_counts`: some device holds exactly 32 live pairs. `members`: each row is a permutation.
All inputs are finite; a program needn't handle non-finite values.
Results may differ from a plain program's by a relative error of at most 0.0095.
Values may be sent and summed in bfloat16 or wider, within the bound.
A program may use at most 64 MiB of HBM per device.

v0:
```python
import math

import jax
import jax.numpy as jnp
from jax import lax
from jax.sharding import PartitionSpec as P

BLK = 128


GELU_K = math.sqrt(2.0 / math.pi)


def from_behind(value, axis, steps):
    count = lax.axis_size(axis)
    first, last = (max(0, -steps), min(count, count - steps))
    return lax.ppermute(value, axis, [(source, source + steps) for source in range(first, last)])


def gelu_tanh(pre_act):
    return (
        0.5
        * pre_act
        * (1.0 + jnp.tanh(GELU_K * (pre_act + 0.044715 * pre_act * pre_act * pre_act)))
    )


def gelu_slope(pre_act):
    tanh_part = jnp.tanh(GELU_K * (pre_act + 0.044715 * pre_act * pre_act * pre_act))
    inner = GELU_K * (1.0 + 3.0 * 0.044715 * pre_act * pre_act)
    return 0.5 * (1.0 + tanh_part) + 0.5 * pre_act * (1.0 - tanh_part * tanh_part) * inner


def normalize(state_rows, norm_gain):
    factor = lax.rsqrt(jnp.mean(state_rows * state_rows, axis=-1, keepdims=True) + 1e-06)
    return state_rows * factor * norm_gain


def norm_backward(state_rows, norm_gain, upstream):
    factor = lax.rsqrt(jnp.mean(state_rows * state_rows, axis=-1, keepdims=True) + 1e-06)
    scaled = upstream * norm_gain
    inner = jnp.mean(state_rows * scaled, axis=-1, keepdims=True)
    return factor * scaled - state_rows * factor * factor * factor * inner


def block_means(normed):
    width = normed.shape[1]
    summed = jnp.sum(normed.astype(jnp.float32).reshape(-1, BLK, width), axis=1)
    return (summed / BLK).astype(jnp.bfloat16)


def spread_blocks(values):
    count = values.shape[0]
    width = values.shape[1]
    return jnp.broadcast_to((values / BLK)[:, None, :], (count, BLK, width)).reshape(
        count * BLK, width
    )


def pick_group():
    for candidate in (16, 8, 4, 2, 1):
        return candidate
    return 1


def run_sides(recv_blocks, grad_blocks, send_proj, recv_ids, send_ids, live_flags, w_recv, w_out):
    block_count = recv_blocks.shape[0]
    block_rows = recv_blocks.shape[1]
    width = recv_blocks.shape[2]
    send_count = send_proj.shape[0]
    hid_dev = w_recv.shape[1]
    side_count = recv_ids.shape[0]
    group_size = pick_group()
    step_count = side_count // group_size
    inputs_all = (
        recv_ids.reshape(step_count, group_size),
        send_ids.reshape(step_count, group_size),
        live_flags.reshape(step_count, group_size),
    )
    contract_rows = (((0,), (0,)), ((), ()))

    def visit(carry, inputs):
        messages, row_grads, proj_grads, grad_recv, grad_out = carry
        recv_idx, send_idx, live_now = inputs
        recv_hot = (recv_idx[:, None] == jnp.arange(block_count, dtype=jnp.int32)[None, :]).astype(
            jnp.float32
        )
        send_hot = (send_idx[:, None] == jnp.arange(send_count, dtype=jnp.int32)[None, :]).astype(
            jnp.float32
        )
        recv_rows = jnp.take(recv_blocks, recv_idx, axis=0).reshape(group_size * block_rows, width)
        grad_rows = jnp.take(grad_blocks, recv_idx, axis=0).reshape(group_size * block_rows, width)
        send_vec = jnp.dot(send_hot, send_proj, precision=lax.Precision.HIGHEST)
        keep_mask = live_now.astype(jnp.bfloat16)[:, None, None]
        pre_act = jnp.dot(recv_rows, w_recv, preferred_element_type=jnp.float32).reshape(
            group_size, block_rows, hid_dev
        )
        pre_act = pre_act + send_vec[:, None, :]
        act_rows = (gelu_tanh(pre_act).astype(jnp.bfloat16) * keep_mask).reshape(-1, hid_dev)
        message = jnp.dot(act_rows, w_out, preferred_element_type=jnp.float32)
        d_act = jnp.dot(grad_rows, w_out.T, preferred_element_type=jnp.float32).reshape(
            group_size, block_rows, hid_dev
        )
        d_pre = (d_act * gelu_slope(pre_act)).astype(jnp.bfloat16) * keep_mask
        grad_vec = jnp.sum(d_pre, axis=1, dtype=jnp.float32)
        d_pre = d_pre.reshape(-1, hid_dev)
        grad_out = grad_out + lax.dot_general(
            act_rows, grad_rows, contract_rows, preferred_element_type=jnp.float32
        )
        grad_recv = grad_recv + lax.dot_general(
            recv_rows, d_pre, contract_rows, preferred_element_type=jnp.float32
        )
        grad_in = jnp.dot(d_pre, w_recv.T, preferred_element_type=jnp.float32)
        messages = messages + jnp.dot(
            recv_hot.T, message.reshape(group_size, -1), precision=lax.Precision.HIGHEST
        )
        row_grads = row_grads + jnp.dot(
            recv_hot.T, grad_in.reshape(group_size, -1), precision=lax.Precision.HIGHEST
        )
        proj_grads = proj_grads + jnp.dot(send_hot.T, grad_vec, precision=lax.Precision.HIGHEST)
        return ((messages, row_grads, proj_grads, grad_recv, grad_out), None)

    initial = (
        jnp.zeros((block_count, block_rows * width), jnp.float32),
        jnp.zeros((block_count, block_rows * width), jnp.float32),
        jnp.zeros((send_count, hid_dev), jnp.float32),
        jnp.zeros((width, hid_dev), jnp.float32),
        jnp.zeros((hid_dev, width), jnp.float32),
    )
    carry, unused = lax.scan(visit, initial, inputs_all)
    messages, row_grads, proj_grads, grad_recv, grad_out = carry
    messages = messages.reshape(block_count * block_rows, width)
    row_grads = row_grads.reshape(block_count * block_rows, width)
    return (messages, row_grads, proj_grads, grad_recv, grad_out)


def on_device(
    agent_state, members, norm_gain, w_recv, w_send, w_out, pair_list, pair_counts, cotangent
):
    region = lax.axis_index("space")
    rows_dev = agent_state.shape[0]
    width = agent_state.shape[1]
    blocks_dev = rows_dev // BLK
    slot_count = pair_list.shape[0]
    state_slots = agent_state.astype(jnp.float32)[members[0]]
    normed = normalize(state_slots, norm_gain).astype(jnp.bfloat16)
    summary = block_means(normed)
    base_block = region * blocks_dev
    slot_ids = jnp.arange(slot_count, dtype=jnp.int32)
    eff_live = (slot_ids < pair_counts[0]).astype(jnp.int32)
    sources = pair_list[:, 0]
    targets = pair_list[:, 1]
    next_normed, next_summary, next_grads = from_behind((normed, summary, cotangent), "space", -1)
    wide_normed = jnp.concatenate([normed, next_normed], axis=0)
    wide_summary = jnp.concatenate([summary, next_summary], axis=0)
    wide_grads = jnp.concatenate([cotangent, next_grads], axis=0)
    send_proj = jnp.dot(wide_summary, w_send, preferred_element_type=jnp.float32)
    recv_ids = jnp.clip(jnp.concatenate([targets, sources]) - base_block, 0, 2 * blocks_dev - 1)
    send_ids = jnp.clip(jnp.concatenate([sources, targets]) - base_block, 0, 2 * blocks_dev - 1)
    live_flags = jnp.concatenate([eff_live, eff_live]).astype(jnp.float32)
    messages, row_grads, proj_grads, grad_recv, grad_out = run_sides(
        wide_normed.reshape(2 * blocks_dev, BLK, width),
        wide_grads.reshape(2 * blocks_dev, BLK, width),
        send_proj,
        recv_ids,
        send_ids,
        live_flags,
        w_recv,
        w_out,
    )
    grad_send = jnp.dot(
        wide_summary.astype(jnp.float32).T, proj_grads, precision=lax.Precision.HIGHEST
    )
    summary_grads = jnp.dot(
        proj_grads, w_send.astype(jnp.float32).T, precision=lax.Precision.HIGHEST
    )
    row_grads = row_grads + spread_blocks(summary_grads)
    stacked = jnp.stack([messages, row_grads]).reshape(2, 2, rows_dev, width)
    incoming = from_behind(stacked[:, 1], "space", 1)
    summed = lax.psum_scatter(
        stacked[:, 0] + incoming, ("hidden", "sub"), scatter_dimension=1, tiled=True
    )
    piece_rows = summed.shape[1]
    piece_index = lax.axis_index("hidden") * lax.axis_size("sub") + lax.axis_index("sub")
    own_state = lax.dynamic_slice_in_dim(state_slots, piece_index * piece_rows, piece_rows, 0)
    own_cotangent = lax.dynamic_slice_in_dim(
        cotangent, piece_index * piece_rows, piece_rows, 0
    ).astype(jnp.float32)
    new_state = (own_state + summed[0]).astype(jnp.bfloat16)
    grad_state = norm_backward(own_state, norm_gain, summed[1]) + own_cotangent
    grad_recv, grad_send, grad_out = lax.psum((grad_recv, grad_send, grad_out), ("space", "sub"))
    return (new_state, grad_state, grad_recv, grad_send, grad_out)


def solution(mesh):
    in_specs = (
        P(("groups", "space"), None),
        P(("groups", "space"), None),
        P(),
        P(None, "hidden"),
        P(None, "hidden"),
        P("hidden", None),
        P(("groups", "space", "sub"), None),
        P(("groups", "space", "sub")),
        P(("groups", "space"), None),
    )
    out_specs = (
        P(("groups", "space", "hidden", "sub"), None),
        P(("groups", "space", "hidden", "sub"), None),
        P("groups", "hidden"),
        P("groups", "hidden"),
        P(("groups", "hidden"), None),
    )
    return jax.shard_map(
        on_device, mesh=mesh, in_specs=in_specs, out_specs=out_specs, check_vma=False
    )
```

profile of v0, /device:TPU:0, one launch (start us, length us, event | category | flops | bytes accessed | tf_op | source)
XLA Modules:
  0.0 312.5 jit_solution(12222532527370625989)
XLA Ops:
  9.9 3.5 %gather_fusion.2 = f32[1024,256]{1,0:T(8,128)S(1)} fusion(f32[1024,256]{1,0:T(8,128)S(1)} %convert_element_type.51, s32[1024]{0:T(1024)S(1)} %broadcast_clamp_fusion), kind=kCustom, calls=%fused_computation.2 | custom fusion | bytes 2101248 | tf_op jit(solution)/shard_map/gather | solution.py:145
  20.7 13.3 %collective-permute-done = bf16[1024,256]{1,0:T(8,128)(2,1)} collective-permute-done((bf16[1024,256]{1,0:T(8,128)(2,1)S(1)}, bf16[1024,256]{1,0:T(8,128)(2,1)}, u32[]{:S(2)}, u32[]{:S(2)}) %collective-permute-start) | collective-permute-done | bytes 524320 | tf_op jit(solution)/shard_map/ppermute | solution.py:17
  35.1 9.3 %collective-permute-done.2 = bf16[1024,256]{1,0:T(8,128)(2,1)} collective-permute-done((bf16[1024,256]{1,0:T(8,128)(2,1)S(1)}, bf16[1024,256]{1,0:T(8,128)(2,1)}, u32[]{:S(2)}, u32[]{:S(2)}) %collective-permute-start.2) | collective-permute-done | bytes 524320 | tf_op jit(solution)/shard_map/ppermute | solution.py:17
  45.6 130.3 %while.19 = (s32[]{:T(128)}, f32[16,32768]{1,0:T(8,128)}, f32[16,32768]{1,0:T(8,128)}, f32[16,512]{1,0:T(8,128)S(1)}, f32[256,512]{1,0:T(8,128)}, /*index=5*/f32...) while((s32[]{:T(128)}, f32[16,32768]{1,0:T(8,128)}, ...), condition=%wide.region_4.6_spmd.clone, body=%wide.region_2.5_spmd.clone.sunk | while | flops 3466078208 | bytes 122956928 | solution.py:130
  47.1 4.7 %fusion.90 = (bf16[16,128,512]{2,1,0:T(8,128)(2,1)}, f32[16,128,512]{2,1,0:T(8,128)}) fusion(f32[16,512]{1,0:T(8,128)S(1)} %fusion.88, bf16[16]{0:T(256)(128)(2,1)S(1)} %fusion.89, bf16[256,512]{1,0:T(8,128)(2,1)} %get-tuple-element.318, bf16[16,128,256]{2,1,0:T(8,128)(2,1)S(1)} %gather_fusion, pred[16]{0:T(512)(128)(4,1)S(1)} %get-tuple-element.273), kind=kOutput, calls=%fused_computation.17.clone.1 | convolution fusion | flops 548929536 | bytes 7634992 | tf_op jit(solution)/shard_map/while/body/eval_jaxpr/dot_general | solution.py:95
  52.5 5.6 %convert_reduce_fusion.3 = (f32[16,512]{1,0:T(8,128)S(1)}, bf16[16,128,512]{2,1,0:T(8,128)(2,1)S(1)}) fusion(bf16[16]{0:T(256)(128)(2,1)} %copy-done.33, f32[16,128,512]{2,1,0:T(8,128)} %get-tuple-element.275, f32[16,512]{1,0:T(8,128)S(1)} %fusion.88, bf16[512,256]{1,0:T(8,128)(2,1)} %get-tuple-element.322, ...), kind=kOutput, calls=%fused_computation.15.clone.1 | convolution fusion | flops 561504256 | bytes 7667760 | tf_op jit(solution)/shard_map/while/body/eval_jaxpr/dot_general | solution.py:101
  61.7 4.3 %convolution_add_fusion.7 = f32[16,32768]{1,0:T(8,128)} fusion(f32[16,32768]{1,0:T(8,128)} %reshape.227, f32[16,32768]{1,0:T(8,128)} %get-tuple-element.296, pred[]{:T(512)S(6)} %compare.3, s32[16]{0:T(128)S(1)} %get-tuple-element.272), kind=kOutput, calls=%fused_computation.3.clone.1 | convolution fusion | flops 101712128 | bytes 6291521 | tf_op jit(solution)/shard_map/while/body/eval_jaxpr/dot_general | solution.py:117
  68.3 4.4 %convolution_add_fusion.6 = f32[16,32768]{1,0:T(8,128)} fusion(f32[16,32768]{1,0:T(8,128)} %reshape.226, f32[16,32768]{1,0:T(8,128)} %get-tuple-element.295, pred[]{:T(512)S(6)} %compare.3, s32[16]{0:T(128)S(1)} %get-tuple-element.272), kind=kOutput, calls=%fused_computation.4.clone.1 | convolution fusion | flops 101712128 | bytes 6291521 | tf_op jit(solution)/shard_map/while/body/eval_jaxpr/dot_general | solution.py:114
  74.7 1.7 fusion.94
  77.9 4.7 %fusion.90 = (bf16[16,128,512]{2,1,0:T(8,128)(2,1)}, f32[16,128,512]{2,1,0:T(8,128)}) fusion(f32[16,512]{1,0:T(8,128)S(1)} %fusion.88, bf16[16]{0:T(256)(128)(2,1)S(1)} %fusion.89, bf16[256,512]{1,0:T(8,128)(2,1)} %get-tuple-element.318, bf16[16,128,256]{2,1,0:T(8,128)(2,1)S(1)} %gather_fusion, pred[16]{0:T(512)(128)(4,1)S(1)} %get-tuple-element.273), kind=kOutput, calls=%fused_computation.17.clone.1 | convolution fusion | flops 548929536 | bytes 7634992 | tf_op jit(solution)/shard_map/while/body/eval_jaxpr/dot_general | solution.py:95
  83.3 5.6 %convert_reduce_fusion.3 = (f32[16,512]{1,0:T(8,128)S(1)}, bf16[16,128,512]{2,1,0:T(8,128)(2,1)S(1)}) fusion(bf16[16]{0:T(256)(128)(2,1)} %copy-done.33, f32[16,128,512]{2,1,0:T(8,128)} %get-tuple-element.275, f32[16,512]{1,0:T(8,128)S(1)} %fusion.88, bf16[512,256]{1,0:T(8,128)(2,1)} %get-tuple-element.322, ...), kind=kOutput, calls=%fused_computation.15.clone.1 | convolution fusion | flops 561504256 | bytes 7667760 | tf_op jit(solution)/shard_map/while/body/eval_jaxpr/dot_general | solution.py:101
  92.5 5.0 %convolution_add_fusion.7 = f32[16,32768]{1,0:T(8,128)} fusion(f32[16,32768]{1,0:T(8,128)} %reshape.227, f32[16,32768]{1,0:T(8,128)} %get-tuple-element.296, pred[]{:T(512)S(6)} %compare.3, s32[16]{0:T(128)S(1)} %get-tuple-element.272), kind=kOutput, calls=%fused_computation.3.clone.1 | convolution fusion | flops 101712128 | bytes 6291521 | tf_op jit(solution)/shard_map/while/body/eval_jaxpr/dot_general | solution.py:117
  99.7 5.0 %convolution_add_fusion.6 = f32[16,32768]{1,0:T(8,128)} fusion(f32[16,32768]{1,0:T(8,128)} %reshape.226, f32[16,32768]{1,0:T(8,128)} %get-tuple-element.295, pred[]{:T(512)S(6)} %compare.3, s32[16]{0:T(128)S(1)} %get-tuple-element.272), kind=kOutput, calls=%fused_computation.4.clone.1 | convolution fusion | flops 101712128 | bytes 6291521 | tf_op jit(solution)/shard_map/while/body/eval_jaxpr/dot_general | solution.py:114
  106.8 2.8 fusion.94
  111.1 4.7 %fusion.90 = (bf16[16,128,512]{2,1,0:T(8,128)(2,1)}, f32[16,128,512]{2,1,0:T(8,128)}) fusion(f32[16,512]{1,0:T(8,128)S(1)} %fusion.88, bf16[16]{0:T(256)(128)(2,1)S(1)} %fusion.89, bf16[256,512]{1,0:T(8,128)(2,1)} %get-tuple-element.318, bf16[16,128,256]{2,1,0:T(8,128)(2,1)S(1)} %gather_fusion, pred[16]{0:T(512)(128)(4,1)S(1)} %get-tuple-element.273), kind=kOutput, calls=%fused_computation.17.clone.1 | convolution fusion | flops 548929536 | bytes 7634992 | tf_op jit(solution)/shard_map/while/body/eval_jaxpr/dot_general | solution.py:95
  116.5 5.6 %convert_reduce_fusion.3 = (f32[16,512]{1,0:T(8,128)S(1)}, bf16[16,128,512]{2,1,0:T(8,128)(2,1)S(1)}) fusion(bf16[16]{0:T(256)(128)(2,1)} %copy-done.33, f32[16,128,512]{2,1,0:T(8,128)} %get-tuple-element.275, f32[16,512]{1,0:T(8,128)S(1)} %fusion.88, bf16[512,256]{1,0:T(8,128)(2,1)} %get-tuple-element.322, ...), kind=kOutput, calls=%fused_computation.15.clone.1 | convolution fusion | flops 561504256 | bytes 7667760 | tf_op jit(solution)/shard_map/while/body/eval_jaxpr/dot_general | solution.py:101
  125.7 5.0 %convolution_add_fusion.7 = f32[16,32768]{1,0:T(8,128)} fusion(f32[16,32768]{1,0:T(8,128)} %reshape.227, f32[16,32768]{1,0:T(8,128)} %get-tuple-element.296, pred[]{:T(512)S(6)} %compare.3, s32[16]{0:T(128)S(1)} %get-tuple-element.272), kind=kOutput, calls=%fused_computation.3.clone.1 | convolution fusion | flops 101712128 | bytes 6291521 | tf_op jit(solution)/shard_map/while/body/eval_jaxpr/dot_general | solution.py:117
  132.9 5.0 %convolution_add_fusion.6 = f32[16,32768]{1,0:T(8,128)} fusion(f32[16,32768]{1,0:T(8,128)} %reshape.226, f32[16,32768]{1,0:T(8,128)} %get-tuple-element.295, pred[]{:T(512)S(6)} %compare.3, s32[16]{0:T(128)S(1)} %get-tuple-element.272), kind=kOutput, calls=%fused_computation.4.clone.1 | convolution fusion | flops 101712128 | bytes 6291521 | tf_op jit(solution)/shard_map/while/body/eval_jaxpr/dot_general | solution.py:114
  139.9 2.8 fusion.94
  144.2 4.7 %fusion.90 = (bf16[16,128,512]{2,1,0:T(8,128)(2,1)}, f32[16,128,512]{2,1,0:T(8,128)}) fusion(f32[16,512]{1,0:T(8,128)S(1)} %fusion.88, bf16[16]{0:T(256)(128)(2,1)S(1)} %fusion.89, bf16[256,512]{1,0:T(8,128)(2,1)} %get-tuple-element.318, bf16[16,128,256]{2,1,0:T(8,128)(2,1)S(1)} %gather_fusion, pred[16]{0:T(512)(128)(4,1)S(1)} %get-tuple-element.273), kind=kOutput, calls=%fused_computation.17.clone.1 | convolution fusion | flops 548929536 | bytes 7634992 | tf_op jit(solution)/shard_map/while/body/eval_jaxpr/dot_general | solution.py:95
  149.6 5.6 %convert_reduce_fusion.3 = (f32[16,512]{1,0:T(8,128)S(1)}, bf16[16,128,512]{2,1,0:T(8,128)(2,1)S(1)}) fusion(bf16[16]{0:T(256)(128)(2,1)} %copy-done.33, f32[16,128,512]{2,1,0:T(8,128)} %get-tuple-element.275, f32[16,512]{1,0:T(8,128)S(1)} %fusion.88, bf16[512,256]{1,0:T(8,128)(2,1)} %get-tuple-element.322, ...), kind=kOutput, calls=%fused_computation.15.clone.1 | convolution fusion | flops 561504256 | bytes 7667760 | tf_op jit(solution)/shard_map/while/body/eval_jaxpr/dot_general | solution.py:101
  158.8 5.0 %convolution_add_fusion.7 = f32[16,32768]{1,0:T(8,128)} fusion(f32[16,32768]{1,0:T(8,128)} %reshape.227, f32[16,32768]{1,0:T(8,128)} %get-tuple-element.296, pred[]{:T(512)S(6)} %compare.3, s32[16]{0:T(128)S(1)} %get-tuple-element.272), kind=kOutput, calls=%fused_computation.3.clone.1 | convolution fusion | flops 101712128 | bytes 6291521 | tf_op jit(solution)/shard_map/while/body/eval_jaxpr/dot_general | solution.py:117
  166.1 5.0 %convolution_add_fusion.6 = f32[16,32768]{1,0:T(8,128)} fusion(f32[16,32768]{1,0:T(8,128)} %reshape.226, f32[16,32768]{1,0:T(8,128)} %get-tuple-element.295, pred[]{:T(512)S(6)} %compare.3, s32[16]{0:T(128)S(1)} %get-tuple-element.272), kind=kOutput, calls=%fused_computation.4.clone.1 | convolution fusion | flops 101712128 | bytes 6291521 | tf_op jit(solution)/shard_map/while/body/eval_jaxpr/dot_general | solution.py:114
  173.1 2.8 fusion.94
  176.3 2.9 reshape.164
  183.9 3.8 %collective-permute-start.3 = (f32[2,1024,256]{2,1,0:T(8,128)S(1)}, f32[2,1024,256]{2,1,0:T(8,128)S(1)}, u32[]{:S(2)}, u32[]{:S(2)}) collective-permute-start(f32[2,1024,256]{2,1,0:T(8,128)S(1)} %fusion.31), channel_id=1, source_target_pairs={{0,4},{4,8},{8,12},{1,5},{5,9},{9,13},{2,6},{6,10},{10,14},{3,7},{... | collective-permute-start | bytes 6291464 | tf_op jit(solution)/shard_map/ppermute | solution.py:17
  187.7 43.9 %collective-permute-done.3 = f32[2,1024,256]{2,1,0:T(8,128)S(1)} collective-permute-done((f32[2,1024,256]{2,1,0:T(8,128)S(1)}, f32[2,1024,256]{2,1,0:T(8,128)S(1)}, u32[]{:S(2)}, u32[]{:S(2)}) %collective-permute-start.3) | collective-permute-done | bytes 2097184 | tf_op jit(solution)/shard_map/ppermute | solution.py:17
  234.5 31.3 %reduce-scatter.2.cloned.1.call-done = f32[2,256,256]{2,1,0:T(8,128)} async-done(((f32[2,1024,256]{2,1,0:T(8,128)}), f32[2,256,256]{2,1,0:T(8,128)}) %reduce-scatter.2.cloned.1.call-update) | async-done | bytes 524304 | tf_op jit(solution)/shard_map/reduce_scatter | solution.py:180
  266.9 1.9 convert_add_fusion
  268.8 31.6 %all-reduce.3.cloned.1.call-done = (f32[256,512]{1,0:T(8,128)}, f32[256,512]{1,0:T(8,128)}, f32[512,256]{1,0:T(8,128)}) async-done(((f32[256,512]{1,0:T(8,128)}, f32[256,512]{1,0:T(8,128)}, f32[512,256]{1,0:T(8,128)}), (f32[256,512]{1,0:T(8,128)}, f32[256,512]{1,0:T(8,128)}, f32[512,256]{1,0:T(8,128)})) %all-reduce.3.cloned.1.call-update) | async-done | bytes 1572880 | tf_op jit(solution)/shard_map/psum | solution.py:191
  300.5 1.9 copy.42
  302.4 1.9 copy.43
  (302 shorter events, 59.8 us)
Async XLA Ops:
  8.0 12.6 %copy-start = (bf16[256,512]{1,0:T(8,128)(2,1)S(1)}, bf16[256,512]{1,0:T(8,128)(2,1)}, u32[]{:S(2)}) copy-start(bf16[256,512]{1,0:T(8,128)(2,1)} %param.17) | copy-start | bytes 786436
  8.0 257.8 %reduce-scatter.2.cloned.1.call-start = ((), (), s32[]{:S(2)}) async-start(), calls=%async_computation.1 | async-start | bytes 2621440 | tf_op jit(solution)/shard_map/reduce_scatter | solution.py:180
  13.4 21.7 %copy-start.12 = (f32[1024,256]{1,0:T(8,128)}, f32[1024,256]{1,0:T(8,128)S(1)}, u32[]{:S(2)}) copy-start(f32[1024,256]{1,0:T(8,128)S(1)} %gather_fusion.2) | copy-start | bytes 3145732
  13.9 6.6 %collective-permute-start.1 = (bf16[8,256]{1,0:T(8,128)(2,1)S(1)}, bf16[8,256]{1,0:T(8,128)(2,1)S(1)}, u32[]{:S(2)}, u32[]{:S(2)}) collective-permute-start(bf16[8,256]{1,0:T(8,128)(2,1)S(1)} %multiply_convert_fusion.3), channel_id=1, source_target_pairs={{4,0},{8,4},{12,8},{5,1},{9,5},{13,9},{6,2},{10,6},{14,10},{7,3},{... | collective-permute-start | bytes 12296 | tf_op jit(solution)/shard_map/ppermute | solution.py:17
  15.6 18.4 %collective-permute-start = (bf16[1024,256]{1,0:T(8,128)(2,1)S(1)}, bf16[1024,256]{1,0:T(8,128)(2,1)}, u32[]{:S(2)}, u32[]{:S(2)}) collective-permute-start(bf16[1024,256]{1,0:T(8,128)(2,1)S(1)} %multiply_convert_fusion.2), channel_id=1, source_target_pairs={{4,0},{8,4},{12,8},{5,1},{9,5},{13,9},{6,2},{10,6},{14,10},{7,3},{... | collective-permute-start | bytes 1572872 | tf_op jit(solution)/shard_map/ppermute | solution.py:17
  16.9 27.5 %collective-permute-start.2 = (bf16[1024,256]{1,0:T(8,128)(2,1)S(1)}, bf16[1024,256]{1,0:T(8,128)(2,1)}, u32[]{:S(2)}, u32[]{:S(2)}) collective-permute-start(bf16[1024,256]{1,0:T(8,128)(2,1)S(1)} %copy-done.18), channel_id=1, source_target_pairs={{4,0},{8,4},{12,8},{5,1},{9,5},{13,9},{6,2},{10,6},{14,10},{7,3},{... | collective-permute-start | bytes 1572872 | tf_op jit(solution)/shard_map/ppermute | solution.py:17
  45.7 6.2 %copy-start.28 = (s32[4,16]{1,0:T(4,128)}, s32[4,16]{1,0:T(4,128)S(1)}, u32[]{:S(2)}) copy-start(s32[4,16]{1,0:T(4,128)S(1)} %get-tuple-element.319) | copy-start | bytes 772 | tf_op jit(solution)/shard_map/while
  45.7 6.2 %copy-start.31 = (bf16[4,16]{1,0:T(4,128)(2,1)}, bf16[4,16]{1,0:T(4,128)(2,1)S(1)}, u32[]{:S(2)}) copy-start(bf16[4,16]{1,0:T(4,128)(2,1)S(1)} %get-tuple-element.321) | copy-start | bytes 388 | tf_op jit(solution)/shard_map/while
  45.7 6.2 %copy-start.6 = (bf16[16,128,256]{2,1,0:T(8,128)(2,1)}, bf16[16,128,256]{2,1,0:T(8,128)(2,1)S(1)}, u32[]{:S(2)}) copy-start(bf16[16,128,256]{2,1,0:T(8,128)(2,1)S(1)} %get-tuple-element.323) | copy-start | bytes 3145732 | tf_op jit(solution)/shard_map/while
  45.7 6.1 %copy-start.24 = (pred[16]{0:T(512)(128)(4,1)}, pred[16]{0:T(512)(128)(4,1)S(1)}, u32[]{:S(2)}) copy-start(pred[16]{0:T(512)(128)(4,1)S(1)} %get-tuple-element.273) | copy-start | bytes 52 | tf_op jit(solution)/shard_map/while
  52.5 6.9 %copy-start.16 = (bf16[256,512]{1,0:T(8,128)(2,1)S(1)}, bf16[256,512]{1,0:T(8,128)(2,1)}, u32[]{:S(2)}) copy-start(bf16[256,512]{1,0:T(8,128)(2,1)} %get-tuple-element.318) | copy-start | bytes 786436 | tf_op jit(solution)/shard_map/while
  76.4 6.2 %copy-start.28 = (s32[4,16]{1,0:T(4,128)}, s32[4,16]{1,0:T(4,128)S(1)}, u32[]{:S(2)}) copy-start(s32[4,16]{1,0:T(4,128)S(1)} %get-tuple-element.319) | copy-start | bytes 772 | tf_op jit(solution)/shard_map/while
  76.5 6.2 %copy-start.31 = (bf16[4,16]{1,0:T(4,128)(2,1)}, bf16[4,16]{1,0:T(4,128)(2,1)S(1)}, u32[]{:S(2)}) copy-start(bf16[4,16]{1,0:T(4,128)(2,1)S(1)} %get-tuple-element.321) | copy-start | bytes 388 | tf_op jit(solution)/shard_map/while
  76.5 6.2 %copy-start.6 = (bf16[16,128,256]{2,1,0:T(8,128)(2,1)}, bf16[16,128,256]{2,1,0:T(8,128)(2,1)S(1)}, u32[]{:S(2)}) copy-start(bf16[16,128,256]{2,1,0:T(8,128)(2,1)S(1)} %get-tuple-element.323) | copy-start | bytes 3145732 | tf_op jit(solution)/shard_map/while
  76.5 6.1 %copy-start.24 = (pred[16]{0:T(512)(128)(4,1)}, pred[16]{0:T(512)(128)(4,1)S(1)}, u32[]{:S(2)}) copy-start(pred[16]{0:T(512)(128)(4,1)S(1)} %get-tuple-element.273) | copy-start | bytes 52 | tf_op jit(solution)/shard_map/while
  83.3 6.9 %copy-start.16 = (bf16[256,512]{1,0:T(8,128)(2,1)S(1)}, bf16[256,512]{1,0:T(8,128)(2,1)}, u32[]{:S(2)}) copy-start(bf16[256,512]{1,0:T(8,128)(2,1)} %get-tuple-element.318) | copy-start | bytes 786436 | tf_op jit(solution)/shard_map/while
  109.6 6.2 %copy-start.28 = (s32[4,16]{1,0:T(4,128)}, s32[4,16]{1,0:T(4,128)S(1)}, u32[]{:S(2)}) copy-start(s32[4,16]{1,0:T(4,128)S(1)} %get-tuple-element.319) | copy-start | bytes 772 | tf_op jit(solution)/shard_map/while
  109.6 6.2 %copy-start.31 = (bf16[4,16]{1,0:T(4,128)(2,1)}, bf16[4,16]{1,0:T(4,128)(2,1)S(1)}, u32[]{:S(2)}) copy-start(bf16[4,16]{1,0:T(4,128)(2,1)S(1)} %get-tuple-element.321) | copy-start | bytes 388 | tf_op jit(solution)/shard_map/while
  109.6 6.2 %copy-start.6 = (bf16[16,128,256]{2,1,0:T(8,128)(2,1)}, bf16[16,128,256]{2,1,0:T(8,128)(2,1)S(1)}, u32[]{:S(2)}) copy-start(bf16[16,128,256]{2,1,0:T(8,128)(2,1)S(1)} %get-tuple-element.323) | copy-start | bytes 3145732 | tf_op jit(solution)/shard_map/while
  109.7 6.1 %copy-start.24 = (pred[16]{0:T(512)(128)(4,1)}, pred[16]{0:T(512)(128)(4,1)S(1)}, u32[]{:S(2)}) copy-start(pred[16]{0:T(512)(128)(4,1)S(1)} %get-tuple-element.273) | copy-start | bytes 52 | tf_op jit(solution)/shard_map/while
  116.5 5.6 %copy-start.8 = (bf16[16,128,256]{2,1,0:T(8,128)(2,1)}, bf16[16,128,256]{2,1,0:T(8,128)(2,1)S(1)}, u32[]{:S(2)}) copy-start(bf16[16,128,256]{2,1,0:T(8,128)(2,1)S(1)} %gather_fusion.1) | copy-start | bytes 3145732 | tf_op jit(solution)/shard_map/while
  116.5 6.9 %copy-start.16 = (bf16[256,512]{1,0:T(8,128)(2,1)S(1)}, bf16[256,512]{1,0:T(8,128)(2,1)}, u32[]{:S(2)}) copy-start(bf16[256,512]{1,0:T(8,128)(2,1)} %get-tuple-element.318) | copy-start | bytes 786436 | tf_op jit(solution)/shard_map/while
  142.8 6.2 %copy-start.28 = (s32[4,16]{1,0:T(4,128)}, s32[4,16]{1,0:T(4,128)S(1)}, u32[]{:S(2)}) copy-start(s32[4,16]{1,0:T(4,128)S(1)} %get-tuple-element.319) | copy-start | bytes 772 | tf_op jit(solution)/shard_map/while
  142.8 6.2 %copy-start.31 = (bf16[4,16]{1,0:T(4,128)(2,1)}, bf16[4,16]{1,0:T(4,128)(2,1)S(1)}, u32[]{:S(2)}) copy-start(bf16[4,16]{1,0:T(4,128)(2,1)S(1)} %get-tuple-element.321) | copy-start | bytes 388 | tf_op jit(solution)/shard_map/while
  142.8 6.2 %copy-start.6 = (bf16[16,128,256]{2,1,0:T(8,128)(2,1)}, bf16[16,128,256]{2,1,0:T(8,128)(2,1)S(1)}, u32[]{:S(2)}) copy-start(bf16[16,128,256]{2,1,0:T(8,128)(2,1)S(1)} %get-tuple-element.323) | copy-start | bytes 3145732 | tf_op jit(solution)/shard_map/while
  142.8 6.1 %copy-start.24 = (pred[16]{0:T(512)(128)(4,1)}, pred[16]{0:T(512)(128)(4,1)S(1)}, u32[]{:S(2)}) copy-start(pred[16]{0:T(512)(128)(4,1)S(1)} %get-tuple-element.273) | copy-start | bytes 52 | tf_op jit(solution)/shard_map/while
  149.6 5.6 %copy-start.8 = (bf16[16,128,256]{2,1,0:T(8,128)(2,1)}, bf16[16,128,256]{2,1,0:T(8,128)(2,1)S(1)}, u32[]{:S(2)}) copy-start(bf16[16,128,256]{2,1,0:T(8,128)(2,1)S(1)} %gather_fusion.1) | copy-start | bytes 3145732 | tf_op jit(solution)/shard_map/while
  149.6 6.9 %copy-start.16 = (bf16[256,512]{1,0:T(8,128)(2,1)S(1)}, bf16[256,512]{1,0:T(8,128)(2,1)}, u32[]{:S(2)}) copy-start(bf16[256,512]{1,0:T(8,128)(2,1)} %get-tuple-element.318) | copy-start | bytes 786436 | tf_op jit(solution)/shard_map/while
  183.9 47.6 %collective-permute-start.3 = (f32[2,1024,256]{2,1,0:T(8,128)S(1)}, f32[2,1024,256]{2,1,0:T(8,128)S(1)}, u32[]{:S(2)}, u32[]{:S(2)}) collective-permute-start(f32[2,1024,256]{2,1,0:T(8,128)S(1)} %fusion.31), channel_id=1, source_target_pairs={{0,4},{4,8},{8,12},{1,5},{5,9},{9,13},{2,6},{6,10},{10,14},{3,7},{... | collective-permute-start | bytes 6291464 | tf_op jit(solution)/shard_map/ppermute | solution.py:17
  233.2 32.6 %copy-start.13 = (f32[1024,256]{1,0:T(8,128)S(1)}, f32[1024,256]{1,0:T(8,128)}, u32[]{:S(2)}) copy-start(f32[1024,256]{1,0:T(8,128)} %copy-done.12) | copy-start | bytes 3145732
  233.2 32.6 %copy-start.23 = (f32[256]{0:T(256)S(1)}, f32[256]{0:T(256)}, u32[]{:S(2)}) copy-start(f32[256]{0:T(256)} %param.15) | copy-start | bytes 3076
  233.2 67.3 %all-reduce.3.cloned.1.call-start = ((), (), s32[]{:S(2)}) async-start(), calls=%async_computation.2 | async-start | bytes 3145728 | tf_op jit(solution)/shard_map/psum | solution.py:191
  (77 other events, 255.9 us)
Sparse Core Ops, SparseCore 0:
  233.3 32.4 reduce-scatter.1
Sparse Core Ops, SparseCore 1:
  237.0 63.4 all-reduce.2
where the time goes:
time: 313 us; the launch traced here: 312 us
  waiting for transfers between devices  131 us (42%)
  matrix products  104 us (33%)
  local copies, waits for them, and re-layouts  42.4 us (14%)
  between operations  16.4 us (5%)
  other arithmetic  10.1 us (3%)
  starting transfers between devices  7.86 us (3%)
    ppermute x4, waiting for transfers between devices, from_behind(): lax.ppermute(value, axis, [(source, source + steps) for source in range(f...  67.8 us
    psum x1, waiting for transfers between devices, on_device(): lax.psum((grad_recv, grad_send, grad_out), ('space', 'sub'))  31.6 us
    reduce_scatter x1, waiting for transfers between devices, on_device(): lax.psum_scatter(stacked[:, 0] + incoming, ('hidden', 'sub'), scatter_dim...  31.3 us
    dot_general x4, matrix products, visit(): jnp.dot(grad_rows, w_out.T, preferred_element_type=jnp.float32)  22.3 us
    dot_general x4, matrix products, visit(): jnp.dot(recv_hot.T, message.reshape(group_size, -1), precision=lax.Precis...  19.4 us
    dot_general x4, matrix products, visit(): jnp.dot(recv_hot.T, grad_in.reshape(group_size, -1), precision=lax.Precis...  19.3 us
    dot_general x4, matrix products, visit(): jnp.dot(recv_rows, w_recv, preferred_element_type=jnp.float32)  18.9 us
    dot_general x4, matrix products, visit(): lax.dot_general(act_rows, grad_rows, contract_rows, preferred_element_typ...  10.1 us
  transfers between devices with their start and end apart: 6, of which 6 were waited for; matrix products, arithmetic and copies ran while one was open for 2% of the time, Pallas kernels for 0%

commit v1 on v0

v1 whole, which is shorter than its diff:
```python
import functools
import math

import jax
import jax.numpy as jnp
from jax import lax
from jax.experimental import pallas as pl
from jax.experimental.pallas import tpu as pltpu
from jax.sharding import PartitionSpec as P

BLK = 128
CHUNK = 16
BF16 = jnp.bfloat16
F32 = jnp.float32
MESH = pl.DeviceIdType.MESH
HIGH = lax.Precision.HIGHEST

GELU_K = math.sqrt(2.0 / math.pi)
BETA = (GELU_K * 0.044715) ** (1.0 / 3.0)
KAPPA = GELU_K / BETA


def dot(a, b, dims=((1,), (0,)), precision=None):
    return lax.dot_general(
        a, b, (dims, ((), ())), preferred_element_type=F32, precision=precision
    )


def kernel(
    dims,
    state_ref,
    memb_ref,
    gain_ref,
    wr_ref,
    ws_ref,
    wo_ref,
    pairs_ref,
    counts_ref,
    cot_ref,
    new_ref,
    gst_ref,
    gr_ref,
    gs_ref,
    go_ref,
    x_buf,
    xs_buf,
    lists,
    win,
    proj,
    mask,
    pre_buf,
    dact_buf,
    a_buf,
    d_buf,
    pg_buf,
    msg_send,
    msg_recv,
    own_msg,
    sg_loc,
    sg_near,
    sg_reg,
    sg_peer,
    w_loc,
    w_send,
    w_recv,
    w_all,
    list_ss,
    list_rs,
    win_ss,
    win_rs,
    msg_ss,
    msg_rs,
    near_ss,
    near_rs,
    peer_ss,
    peer_rs,
    red_ss,
    red_rs,
    gat_ss,
    gat_rs,
    fwd_ss,
    fwd_rs,
):
    nz, nh, ns = dims
    rows, width = state_ref.shape
    blocks = rows // BLK
    slots = pairs_ref.shape[0]
    quarter = wr_ref.shape[1] // ns
    owners = nh * ns
    own_blocks = blocks // owners
    piece = own_blocks * BLK
    r = lax.axis_index("space")
    h = lax.axis_index("hidden")
    s = lax.axis_index("sub")
    after = lax.rem(r + 1, nz)
    before = lax.rem(r + nz - 1, nz)

    def peer(dh, ds):
        return lax.rem(h + dh, nh), lax.rem(s + ds, ns)

    offsets = [(dh, ds) for dh in range(nh - 1, -1, -1) for ds in range(ns - 1, -1, -1)]

    barrier = pltpu.get_barrier_semaphore()
    met = 0
    for k in range(1, nz):
        pl.semaphore_signal(
            barrier, inc=1, device_id={"space": lax.rem(r + k, nz)}, device_id_type=MESH
        )
        met += 1
    for dh, ds in offsets[:-1]:
        ph, ps = peer(dh, ds)
        pl.semaphore_signal(
            barrier, inc=1, device_id={"hidden": ph, "sub": ps}, device_id_type=MESH
        )
        met += 1
    for ds in range(1, ns):
        for other in (after, before):
            pl.semaphore_signal(
                barrier,
                inc=1,
                device_id={"space": other, "sub": lax.rem(s + ds, ns)},
                device_id_type=MESH,
            )
            met += 1

    live = lax.broadcasted_iota(jnp.int32, (slots, 128), 0) < counts_ref[0]
    for column in range(2):
        ids = jnp.broadcast_to(pairs_ref[:, column : column + 1], (slots, 128))
        lists[0, column * slots : (column + 1) * slots, :] = jnp.where(live, ids, -1000000)

    gain = gain_ref[...]
    for k in range(rows // 256):
        hot = lax.broadcasted_iota(jnp.int32, (rows, 256), 0) == memb_ref[:, k * 256 : (k + 1) * 256]
        xs = dot(hot.astype(F32).astype(BF16), state_ref[...], ((0,), (0,)))
        factor = lax.rsqrt(jnp.mean(xs * xs, axis=-1, keepdims=True) + 1e-06)
        normed = (xs * factor * gain).astype(BF16)
        x_buf[k * 256 : (k + 1) * 256, :] = normed
        xs_buf[k * 256 : (k + 1) * 256, :] = xs.astype(BF16)
        means = jnp.sum(normed.astype(F32).reshape(256 // BLK, BLK, width), axis=1) / BLK
        first = blocks + k * (256 // BLK)
        win[first : first + 256 // BLK, :] = means.astype(BF16).astype(F32)

    pl.semaphore_wait(barrier, met)

    copies = []

    def send(src, dst, ss, rs, where):
        copy = pltpu.make_async_remote_copy(
            src_ref=src,
            dst_ref=dst,
            send_sem=ss,
            recv_sem=rs,
            device_id=where,
            device_id_type=MESH,
        )
        copy.start()
        return copy

    for n, (other, place) in enumerate(((before, 2 * blocks), (after, 0))):
        copies.append(
            send(
                win.at[pl.ds(blocks, blocks)],
                win.at[pl.ds(place, blocks)],
                win_ss.at[n],
                win_rs.at[n],
                {"space": other},
            )
        )
    for ds in range(1, ns):
        copies.append(
            send(
                lists.at[0],
                lists.at[ds],
                list_ss.at[ds - 1],
                list_rs.at[ds - 1],
                {"sub": lax.rem(s + ds, ns)},
            )
        )
    for ds in range(ns):
        copies.append(
            send(
                lists.at[0],
                lists.at[ns + ds],
                list_ss.at[ns - 1 + ds],
                list_rs.at[ns - 1 + ds],
                {"space": after, "sub": lax.rem(s + ds, ns)},
            )
        )

    own_cols = pl.ds(pl.multiple_of(s * quarter, quarter), quarter)
    wr = wr_ref[:, own_cols]
    wo = wo_ref[own_cols, :]
    ws = ws_ref[:, own_cols]
    for k in range(rows // 256):
        part = slice(k * 256, (k + 1) * 256)
        pre_buf[part, :] = dot(x_buf[part, :], wr) * BETA
        dact_buf[part, :] = dot(cot_ref[part, :], wo, ((1,), (1,)))
    pg_buf[...] = jnp.zeros_like(pg_buf)

    for copy in copies:
        copy.wait()

    span = 4 * blocks
    base = r * blocks
    marks = []
    lane = lax.broadcasted_iota(jnp.int32, (slots, 128), 1)
    for n in range(2 * ns):
        source = lists[n, 0:slots, :] - base
        target = lists[n, slots : 2 * slots, :] - base
        for recv, sender in ((target, source), (source, target)):
            inside = (recv >= 0) & (recv < blocks)
            place = jnp.where(inside, recv * span + (sender - recv + blocks), -1)
            marks.append(
                jnp.concatenate(
                    [
                        (place == lane + c * 128).astype(F32).astype(BF16)
                        for c in range(blocks * span // 128)
                    ],
                    axis=1,
                )
            )
    marks = jnp.concatenate(marks, axis=0)
    mask[...] = dot(marks, jnp.ones((marks.shape[0], quarter), BF16), ((0,), (0,)))
    proj[...] = dot(win[...].astype(BF16), ws) * BETA

    def one_block(a):
        def one_chunk(c, carry):
            here = pl.ds(pl.multiple_of(a * BLK + c * CHUNK, CHUNK), CHUNK)
            v0 = pre_buf[here, :]
            da = dact_buf[here, :]
            act_sum = jnp.zeros((CHUNK, quarter), F32)
            d_sum = jnp.zeros((CHUNK, quarter), F32)
            for d in range(2 * blocks + 1):
                if d == blocks:
                    continue
                v = v0 + proj[pl.ds(a + d, 1), :]
                v2 = v * v
                t = jnp.tanh(v * (v2 + KAPPA))
                rise = (1.0 + t) * mask[pl.ds(a * span + d, 1), :]
                act = v * rise
                act_sum = act_sum + act
                slope = rise + act * (1.0 - t) * (3.0 * v2 + KAPPA)
                d_pre = da * slope
                d_sum = d_sum + d_pre
                pg = pl.ds(pl.multiple_of((a + d) * 8, 8), 8)
                total = d_pre[0:8, :]
                for i in range(1, CHUNK // 8):
                    total = total + d_pre[i * 8 : (i + 1) * 8, :]
                pg_buf[pg, :] = pg_buf[pg, :] + total
            a_buf[here, :] = (act_sum * (0.5 / BETA)).astype(BF16)
            d_buf[here, :] = (d_sum * 0.5).astype(BF16)
            return carry

        lax.fori_loop(0, BLK // CHUNK, one_chunk, 0)

    msg_copies = []
    for n, (dh, ds) in enumerate(offsets):
        ph, ps = peer(dh, ds)
        first = (ph * ns + ps) * own_blocks

        def step(i, carry, first=first):
            one_block(first + i)
            return carry

        lax.fori_loop(0, own_blocks, step, 0)
        here = pl.ds(pl.multiple_of(first * BLK, BLK), piece)
        message = dot(a_buf[here, :], wo)
        grads = dot(d_buf[here, :], wr, ((1,), (1,)))
        if n < owners - 1:
            msg_send[n, 0:piece, :] = message.astype(BF16)
            msg_send[n, piece : 2 * piece, :] = grads.astype(BF16)
            msg_copies.append(
                send(
                    msg_send.at[n],
                    msg_recv.at[n],
                    msg_ss.at[n],
                    msg_rs.at[n],
                    {"hidden": ph, "sub": ps},
                )
            )
        else:
            own_msg[0:piece, :] = message
            own_msg[piece : 2 * piece, :] = grads

    pg = jnp.sum(pg_buf[...].reshape(3 * blocks, 8, quarter), axis=1) * 0.5
    sg_loc[...] = dot(pg, ws.astype(F32), ((1,), (1,)), HIGH)
    near = [
        send(
            sg_loc.at[pl.ds(place, blocks)],
            sg_near.at[n],
            near_ss.at[n],
            near_rs.at[n],
            {"space": other},
        )
        for n, (other, place) in enumerate(((before, 0), (after, 2 * blocks)))
    ]

    w_loc[0:width, :] = dot(x_buf[...], d_buf[...], ((0,), (0,)))
    w_loc[width : 2 * width, :] = dot(win[...], pg, ((0,), (0,)), HIGH)
    for c in range(width // quarter):
        w_loc[2 * width + c * quarter : 2 * width + (c + 1) * quarter, :] = dot(
            a_buf[...], cot_ref[:, c * quarter : (c + 1) * quarter], ((0,), (0,))
        )
    travel = w_send.dtype
    w_send[...] = w_loc[...].astype(travel)
    share = 3 * width // nz

    def share_at(index):
        return pl.ds(pl.multiple_of(index * share, share), share)

    reduces = []
    for k in range(1, nz):
        to = lax.rem(r + k, nz)
        reduces.append(
            send(
                w_send.at[share_at(to)],
                w_recv.at[k - 1],
                red_ss.at[k - 1],
                red_rs.at[k - 1],
                {"space": to},
            )
        )

    for copy in near:
        copy.wait()
    sg_reg[...] = sg_loc[blocks : 2 * blocks, :] + sg_near[0] + sg_near[1]
    peers = []
    for n, (dh, ds) in enumerate(offsets[:-1]):
        ph, ps = peer(dh, ds)
        peers.append(
            send(
                sg_reg,
                sg_peer.at[n],
                peer_ss.at[n],
                peer_rs.at[n],
                {"hidden": ph, "sub": ps},
            )
        )

    for copy in reduces:
        copy.wait_recv()
    total = w_loc[share_at(r), :]
    for k in range(1, nz):
        total = total + w_recv[k - 1].astype(F32)
    w_all[0, share_at(r), :] = total.astype(travel)
    gathers = []
    forwards = []
    for k in range(1, nz):
        gathers.append(
            send(
                w_all.at[0, share_at(r)],
                w_all.at[0, share_at(r)],
                gat_ss.at[k - 1],
                gat_rs.at[k - 1],
                {"space": lax.rem(r + k, nz)},
            )
        )

    def forward(k):
        origin = share_at(lax.rem(r + nz - k, nz))
        for ds in range(1, ns):
            forwards.append(
                send(
                    w_all.at[0, origin],
                    w_all.at[ds, origin],
                    fwd_ss.at[ds - 1, k],
                    fwd_rs.at[ds - 1, k],
                    {"sub": lax.rem(s + ds, ns)},
                )
            )

    forward(0)

    for copy in msg_copies:
        copy.wait()
    for copy in peers:
        copy.wait()
    message = own_msg[0:piece, :]
    grads = own_msg[piece : 2 * piece, :]
    near_sum = sg_reg[...]
    for n in range(owners - 1):
        message = message + msg_recv[n, 0:piece, :].astype(F32)
        grads = grads + msg_recv[n, piece : 2 * piece, :].astype(F32)
        near_sum = near_sum + sg_peer[n]
    sg_loc[0:blocks, :] = near_sum / BLK
    q = h * ns + s
    mine = pl.ds(pl.multiple_of(q * piece, piece), piece)
    xs = xs_buf[mine, :].astype(F32)
    new_ref[...] = (xs + message).astype(BF16)
    spread = jnp.concatenate(
        [
            jnp.broadcast_to(sg_loc[pl.ds(q * own_blocks + i, 1), :], (BLK, width))
            for i in range(own_blocks)
        ],
        axis=0,
    )
    factor = lax.rsqrt(jnp.mean(xs * xs, axis=-1, keepdims=True) + 1e-06)
    scaled = (grads + spread) * gain
    inner = jnp.mean(xs * scaled, axis=-1, keepdims=True)
    gst_ref[...] = (
        factor * scaled - xs * factor * factor * factor * inner + cot_ref[mine, :].astype(F32)
    )

    for k in range(1, nz):
        gathers[k - 1].wait_recv()
        forward(k)
    for copy in forwards:
        copy.wait_recv()
    for ds in range(ns):
        begin = pl.multiple_of(lax.rem(s + ns - ds, ns) * quarter, quarter)
        cols = pl.ds(begin, quarter)
        gr_ref[:, cols] = w_all[ds, 0:width, :].astype(F32)
        gs_ref[:, cols] = w_all[ds, width : 2 * width, :].astype(F32)
        for c in range(width // quarter):
            at = 2 * width + c * quarter
            go_ref[cols, c * quarter : (c + 1) * quarter] = w_all[ds, at : at + quarter, :].astype(
                F32
            )
    for copy in reduces + gathers + forwards:
        copy.wait_send()


def on_device(
    dims,
    agent_state,
    members,
    norm_gain,
    w_recv,
    w_send,
    w_out,
    pair_list,
    pair_counts,
    cotangent,
):
    nz, nh, ns = dims
    rows, width = agent_state.shape
    blocks = rows // BLK
    slots = pair_list.shape[0]
    hid_dev = w_recv.shape[1]
    quarter = hid_dev // ns
    owners = nh * ns
    piece = rows // owners
    share = 3 * width // nz
    travel = BF16 if share % 16 == 0 else F32
    dma = pltpu.SemaphoreType.DMA
    vmem = pl.BlockSpec(memory_space=pltpu.VMEM)
    smem = pl.BlockSpec(memory_space=pltpu.SMEM)
    return pl.pallas_call(
        functools.partial(kernel, dims),
        out_shape=(
            jax.ShapeDtypeStruct((piece, width), BF16),
            jax.ShapeDtypeStruct((piece, width), F32),
            jax.ShapeDtypeStruct((width, hid_dev), F32),
            jax.ShapeDtypeStruct((width, hid_dev), F32),
            jax.ShapeDtypeStruct((hid_dev, width), F32),
        ),
        in_specs=[vmem] * 7 + [smem, vmem],
        out_specs=(vmem,) * 5,
        scratch_shapes=[
            pltpu.VMEM((rows, width), BF16),
            pltpu.VMEM((rows, width), BF16),
            pltpu.VMEM((2 * ns, 2 * slots, 128), jnp.int32),
            pltpu.VMEM((3 * blocks, width), F32),
            pltpu.VMEM((3 * blocks, quarter), F32),
            pltpu.VMEM((4 * blocks * blocks, quarter), F32),
            pltpu.VMEM((rows, quarter), F32),
            pltpu.VMEM((rows, quarter), F32),
            pltpu.VMEM((rows, quarter), BF16),
            pltpu.VMEM((rows, quarter), BF16),
            pltpu.VMEM((3 * blocks * 8, quarter), F32),
            pltpu.VMEM((owners - 1, 2 * piece, width), BF16),
            pltpu.VMEM((owners - 1, 2 * piece, width), BF16),
            pltpu.VMEM((2 * piece, width), F32),
            pltpu.VMEM((3 * blocks, width), F32),
            pltpu.VMEM((2, blocks, width), F32),
            pltpu.VMEM((blocks, width), F32),
            pltpu.VMEM((owners - 1, blocks, width), F32),
            pltpu.VMEM((3 * width, quarter), F32),
            pltpu.VMEM((3 * width, quarter), travel),
            pltpu.VMEM((nz - 1, share, quarter), travel),
            pltpu.VMEM((ns, 3 * width, quarter), travel),
            dma((2 * ns - 1,)),
            dma((2 * ns - 1,)),
            dma((2,)),
            dma((2,)),
            dma((owners - 1,)),
            dma((owners - 1,)),
            dma((2,)),
            dma((2,)),
            dma((owners - 1,)),
            dma((owners - 1,)),
            dma((nz - 1,)),
            dma((nz - 1,)),
            dma((nz - 1,)),
            dma((nz - 1,)),
            dma((ns - 1, nz)),
            dma((ns - 1, nz)),
        ],
        compiler_params=pltpu.CompilerParams(
            collective_id=0, has_side_effects=True, vmem_limit_bytes=48 * 1024 * 1024
        ),
    )(
        agent_state,
        members,
        norm_gain.reshape(1, width),
        w_recv,
        w_send,
        w_out,
        pair_list,
        pair_counts,
        cotangent,
    )


def solution(mesh):
    in_specs = (
        P(("groups", "space"), None),
        P(("groups", "space"), None),
        P(),
        P(None, "hidden"),
        P(None, "hidden"),
        P("hidden", None),
        P(("groups", "space", "sub"), None),
        P(("groups", "space", "sub")),
        P(("groups", "space"), None),
    )
    out_specs = (
        P(("groups", "space", "hidden", "sub"), None),
        P(("groups", "space", "hidden", "sub"), None),
        P("groups", "hidden"),
        P("groups", "hidden"),
        P(("groups", "hidden"), None),
    )
    dims = (mesh.shape["space"], mesh.shape["hidden"], mesh.shape["sub"])
    return jax.shard_map(
        functools.partial(on_device, dims),
        mesh=mesh,
        in_specs=in_specs,
        out_specs=out_specs,
        check_vma=False,
    )
```

time: 313 us -> 52.5 us (0.17)
  the two profiles are of different devices: /device:TPU:0 before, /device:TPU:25 now
where the time goes in v1:
time: 52.5 us; the launch traced here: 52.1 us
  Pallas kernels  40.8 us (78%)
  local copies, waits for them, and re-layouts  10 us (19%)
  between operations  1.31 us (2%)
    pallas_call x1, Pallas kernels, on_device(): pl.pallas_call(functools.partial(kernel, dims), out_shape=(jax.ShapeDtype...  40.8 us
    unnamed x22, local copies, waits for them, and re-layouts  10 us

profile of v1, /device:TPU:25, one launch (start us, length us, event | category | flops | bytes accessed | tf_op | source)
XLA Modules:
  0.0 52.1 jit_solution(3281257268916105041)
XLA Ops:
  1.3 0.0 copy-start.7
  1.3 0.7 %copy-done.7 = s32[32,2]{0,1:T(2,128)S(1)} copy-done((s32[32,2]{0,1:T(2,128)S(1)}, s32[32,2]{0,1:T(2,128)}, u32[]{:S(2)}) %copy-start.7) | copy-done | bytes 280
  2.0 0.0 copy-start.5
  2.0 0.0 copy-start.6
  2.0 0.1 copy.14.pairs_ref
  2.1 0.6 %copy-done.5 = s32[1,1024]{1,0:T(1,128)S(1)} copy-done((s32[1,1024]{1,0:T(1,128)S(1)}, s32[1,1024]{1,0:T(1,128)}, u32[]{:S(2)}) %copy-start.5) | copy-done | bytes 4120
  2.6 0.0 copy-done.6
  2.7 0.0 copy-start
  2.7 1.0 %copy-done = bf16[1024,256]{1,0:T(8,128)(2,1)S(1)} copy-done((bf16[1024,256]{1,0:T(8,128)(2,1)S(1)}, bf16[1024,256]{1,0:T(8,128)(2,1)}, u32[]{:S(2)}) %copy-start) | copy-done | bytes 524312
  3.7 0.0 copy-start.1
  3.7 1.0 %copy-done.1 = bf16[1024,256]{1,0:T(8,128)(2,1)S(1)} copy-done((bf16[1024,256]{1,0:T(8,128)(2,1)S(1)}, bf16[1024,256]{1,0:T(8,128)(2,1)}, u32[]{:S(2)}) %copy-start.1) | copy-done | bytes 524312
  4.7 0.0 copy-start.2
  4.7 0.9 %copy-done.2 = bf16[256,512]{1,0:T(8,128)(2,1)S(1)} copy-done((bf16[256,512]{1,0:T(8,128)(2,1)S(1)}, bf16[256,512]{1,0:T(8,128)(2,1)}, u32[]{:S(2)}) %copy-start.2) | copy-done | bytes 262168
  5.7 0.0 copy-start.3
  5.7 0.9 %copy-done.3 = bf16[256,512]{1,0:T(8,128)(2,1)S(1)} copy-done((bf16[256,512]{1,0:T(8,128)(2,1)S(1)}, bf16[256,512]{1,0:T(8,128)(2,1)}, u32[]{:S(2)}) %copy-start.3) | copy-done | bytes 262168
  6.6 0.0 copy-start.4
  6.6 0.9 %copy-done.4 = bf16[512,256]{1,0:T(8,128)(2,1)S(1)} copy-done((bf16[512,256]{1,0:T(8,128)(2,1)S(1)}, bf16[512,256]{1,0:T(8,128)(2,1)}, u32[]{:S(2)}) %copy-start.4) | copy-done | bytes 262168
  7.6 40.8 %shard_map.128 = (bf16[256,256]{1,0:T(8,128)(2,1)S(1)}, f32[256,256]{1,0:T(8,128)S(1)}, f32[256,512]{1,0:T(8,128)S(1)}, f32[256,512]{1,0:T(8,128)S(1)}, f32[512,256]{1,0:T(8,128)S(1)}) custom-call(bf16[1024,256]{1,0:T(8,128)(2,1)S(1)} %copy-done, s32[1,1024]{1,0:T(1,128)S(1)} %copy-done.5, f32[1,256]{1,0:T(1,128)S(1)} %bitcast.1, ...), custom_call_target="tpu_custom_call" | custom-call | tf_op jit(solution)/shard_map/pallas_call | solution.py:448
  48.3 0.7 %copy.21 = bf16[256,256]{1,0:T(8,128)(2,1)} copy(bf16[256,256]{1,0:T(8,128)(2,1)S(1)} %get-tuple-element.10) | data formatting | bytes 262144
  49.0 0.7 %copy.22 = f32[256,256]{1,0:T(8,128)} copy(f32[256,256]{1,0:T(8,128)S(1)} %get-tuple-element.11) | data formatting | bytes 524288
  49.7 0.8 %copy.23 = f32[256,512]{1,0:T(8,128)} copy(f32[256,512]{1,0:T(8,128)S(1)} %get-tuple-element.12) | data formatting | bytes 1048576
  50.5 0.8 %copy.24 = f32[256,512]{1,0:T(8,128)} copy(f32[256,512]{1,0:T(8,128)S(1)} %get-tuple-element.13) | data formatting | bytes 1048576
  51.3 0.8 %copy.25 = f32[512,256]{1,0:T(8,128)} copy(f32[512,256]{1,0:T(8,128)S(1)} %get-tuple-element.14) | data formatting | bytes 1048576
Async XLA Ops:
  1.3 0.7 %copy-start.7 = (s32[32,2]{0,1:T(2,128)S(1)}, s32[32,2]{0,1:T(2,128)}, u32[]{:S(2)}) copy-start(s32[32,2]{0,1:T(2,128)} %param.15) | copy-start | bytes 772
  2.0 0.7 %copy-start.5 = (s32[1,1024]{1,0:T(1,128)S(1)}, s32[1,1024]{1,0:T(1,128)}, u32[]{:S(2)}) copy-start(s32[1,1024]{1,0:T(1,128)} %memb_ref.1) | copy-start | bytes 12292
  2.0 0.7 %copy-start.6 = (f32[256]{0:T(256)S(1)}, f32[256]{0:T(256)}, u32[]{:S(2)}) copy-start(f32[256]{0:T(256)} %param.11) | copy-start | bytes 3076
  2.7 1.0 %copy-start = (bf16[1024,256]{1,0:T(8,128)(2,1)S(1)}, bf16[1024,256]{1,0:T(8,128)(2,1)}, u32[]{:S(2)}) copy-start(bf16[1024,256]{1,0:T(8,128)(2,1)} %state_ref.1) | copy-start | bytes 1572868
  3.7 1.0 %copy-start.1 = (bf16[1024,256]{1,0:T(8,128)(2,1)S(1)}, bf16[1024,256]{1,0:T(8,128)(2,1)}, u32[]{:S(2)}) copy-start(bf16[1024,256]{1,0:T(8,128)(2,1)} %cot_ref.1) | copy-start | bytes 1572868
  4.7 0.9 %copy-start.2 = (bf16[256,512]{1,0:T(8,128)(2,1)S(1)}, bf16[256,512]{1,0:T(8,128)(2,1)}, u32[]{:S(2)}) copy-start(bf16[256,512]{1,0:T(8,128)(2,1)} %wr_ref.1) | copy-start | bytes 786436
  5.7 0.9 %copy-start.3 = (bf16[256,512]{1,0:T(8,128)(2,1)S(1)}, bf16[256,512]{1,0:T(8,128)(2,1)}, u32[]{:S(2)}) copy-start(bf16[256,512]{1,0:T(8,128)(2,1)} %ws_ref.1) | copy-start | bytes 786436
  6.6 0.9 %copy-start.4 = (bf16[512,256]{1,0:T(8,128)(2,1)S(1)}, bf16[512,256]{1,0:T(8,128)(2,1)}, u32[]{:S(2)}) copy-start(bf16[512,256]{1,0:T(8,128)(2,1)} %wo_ref.1) | copy-start | bytes 786436

commit v2 on v1

--- a/solution.py
+++ b/solution.py
@@ -28,6 +28,20 @@
 
 def kernel(
     dims,
+    state_hbm,
+    memb_hbm,
+    gain_hbm,
+    wr_hbm,
+    ws_hbm,
+    wo_hbm,
+    pairs_hbm,
+    counts_ref,
+    cot_hbm,
+    new_ref,
+    gst_ref,
+    gr_ref,
+    gs_ref,
+    go_ref,
     state_ref,
     memb_ref,
     gain_ref,
@@ -35,13 +49,7 @@
     ws_ref,
     wo_ref,
     pairs_ref,
-    counts_ref,
     cot_ref,
-    new_ref,
-    gst_ref,
-    gr_ref,
-    gs_ref,
-    go_ref,
     x_buf,
     xs_buf,
     lists,
@@ -64,6 +72,7 @@
     w_send,
     w_recv,
     w_all,
+    in_sem,
     list_ss,
     list_rs,
     win_ss,
@@ -84,8 +93,8 @@
     nz, nh, ns = dims
     rows, width = state_ref.shape
     blocks = rows // BLK
-    slots = pairs_ref.shape[0]
-    quarter = wr_ref.shape[1] // ns
+    slots = pairs_ref.shape[1]
+    quarter = wr_ref.shape[1]
     owners = nh * ns
     own_blocks = blocks // owners
     piece = own_blocks * BLK
@@ -100,6 +109,25 @@
 
     offsets = [(dh, ds) for dh in range(nh - 1, -1, -1) for ds in range(ns - 1, -1, -1)]
 
+    own_cols = pl.ds(pl.multiple_of(s * quarter, quarter), quarter)
+    loads = [
+        pltpu.make_async_copy(src, dst, in_sem.at[n])
+        for n, (src, dst) in enumerate(
+            (
+                (memb_hbm, memb_ref),
+                (state_hbm, state_ref),
+                (gain_hbm, gain_ref),
+                (pairs_hbm, pairs_ref),
+                (wr_hbm.at[:, own_cols], wr_ref),
+                (cot_hbm, cot_ref),
+                (wo_hbm.at[own_cols, :], wo_ref),
+                (ws_hbm.at[:, own_cols], ws_ref),
+            )
+        )
+    ]
+    for load in loads:
+        load.start()
+
     barrier = pltpu.get_barrier_semaphore()
     met = 0
     for k in range(1, nz):
@@ -123,9 +151,17 @@
             )
             met += 1
 
+    for load in loads[:4]:
+        load.wait()
+
     live = lax.broadcasted_iota(jnp.int32, (slots, 128), 0) < counts_ref[0]
+    diagonal = lax.broadcasted_iota(jnp.int32, (slots, slots), 0) == lax.broadcasted_iota(
+        jnp.int32, (slots, slots), 1
+    )
     for column in range(2):
-        ids = jnp.broadcast_to(pairs_ref[:, column : column + 1], (slots, 128))
+        ids = jnp.where(diagonal, pairs_ref[column : column + 1, :].astype(F32), 0.0)
+        ids = jnp.sum(ids, axis=1, keepdims=True).astype(jnp.int32)
+        ids = jnp.broadcast_to(ids, (slots, 128))
         lists[0, column * slots : (column + 1) * slots, :] = jnp.where(live, ids, -1000000)
 
     gain = gain_ref[...]
@@ -187,10 +223,11 @@
             )
         )
 
-    own_cols = pl.ds(pl.multiple_of(s * quarter, quarter), quarter)
-    wr = wr_ref[:, own_cols]
-    wo = wo_ref[own_cols, :]
-    ws = ws_ref[:, own_cols]
+    for load in loads[4:]:
+        load.wait()
+    wr = wr_ref[...]
+    wo = wo_ref[...]
+    ws = ws_ref[...]
     for k in range(rows // 256):
         part = slice(k * 256, (k + 1) * 256)
         pre_buf[part, :] = dot(x_buf[part, :], wr) * BETA
@@ -420,6 +457,25 @@
         copy.wait_send()
 
 
+def store(new_in, gst_in, gr_in, gs_in, go_in, new_out, gst_out, gr_out, gs_out, go_out, sem):
+    copies = [
+        pltpu.make_async_copy(src, dst, sem.at[n])
+        for n, (src, dst) in enumerate(
+            (
+                (gr_in, gr_out),
+                (gs_in, gs_out),
+                (go_in, go_out),
+                (gst_in, gst_out),
+                (new_in, new_out),
+            )
+        )
+    ]
+    for copy in copies:
+        copy.start()
+    for copy in copies:
+        copy.wait()
+
+
 def on_device(
     dims,
     agent_state,
@@ -445,18 +501,28 @@
     dma = pltpu.SemaphoreType.DMA
     vmem = pl.BlockSpec(memory_space=pltpu.VMEM)
     smem = pl.BlockSpec(memory_space=pltpu.SMEM)
-    return pl.pallas_call(
+    hbm = pl.BlockSpec(memory_space=pltpu.HBM)
+    out_shape = (
+        jax.ShapeDtypeStruct((piece, width), BF16),
+        jax.ShapeDtypeStruct((piece, width), F32),
+        jax.ShapeDtypeStruct((width, hid_dev), F32),
+        jax.ShapeDtypeStruct((width, hid_dev), F32),
+        jax.ShapeDtypeStruct((hid_dev, width), F32),
+    )
+    results = pl.pallas_call(
         functools.partial(kernel, dims),
-        out_shape=(
-            jax.ShapeDtypeStruct((piece, width), BF16),
-            jax.ShapeDtypeStruct((piece, width), F32),
-            jax.ShapeDtypeStruct((width, hid_dev), F32),
-            jax.ShapeDtypeStruct((width, hid_dev), F32),
-            jax.ShapeDtypeStruct((hid_dev, width), F32),
-        ),
-        in_specs=[vmem] * 7 + [smem, vmem],
+        out_shape=out_shape,
+        in_specs=[hbm] * 7 + [smem, hbm],
         out_specs=(vmem,) * 5,
         scratch_shapes=[
+            pltpu.VMEM((rows, width), BF16),
+            pltpu.VMEM((1, rows), jnp.int32),
+            pltpu.VMEM((1, width), F32),
+            pltpu.VMEM((width, quarter), BF16),
+            pltpu.VMEM((width, quarter), BF16),
+            pltpu.VMEM((quarter, width), BF16),
+            pltpu.VMEM((2, slots), jnp.int32),
+            pltpu.VMEM((rows, width), BF16),
             pltpu.VMEM((rows, width), BF16),
             pltpu.VMEM((rows, width), BF16),
             pltpu.VMEM((2 * ns, 2 * slots, 128), jnp.int32),
@@ -479,6 +545,7 @@
             pltpu.VMEM((3 * width, quarter), travel),
             pltpu.VMEM((nz - 1, share, quarter), travel),
             pltpu.VMEM((ns, 3 * width, quarter), travel),
+            dma((8,)),
             dma((2 * ns - 1,)),
             dma((2 * ns - 1,)),
             dma((2,)),
@@ -497,7 +564,7 @@
             dma((ns - 1, nz)),
         ],
         compiler_params=pltpu.CompilerParams(
-            collective_id=0, has_side_effects=True, vmem_limit_bytes=48 * 1024 * 1024
+            collective_id=0, has_side_effects=True, vmem_limit_bytes=64 * 1024 * 1024
         ),
     )(
         agent_state,
@@ -506,10 +573,18 @@
         w_recv,
         w_send,
         w_out,
-        pair_list,
+        pair_list.T,
         pair_counts,
         cotangent,
     )
+    return pl.pallas_call(
+        store,
+        out_shape=out_shape,
+        in_specs=[hbm] * 5,
+        out_specs=(hbm,) * 5,
+        scratch_shapes=[dma((5,))],
+        compiler_params=pltpu.CompilerParams(vmem_limit_bytes=64 * 1024 * 1024),
+    )(*results)
 
 
 def solution(mesh):

time: 52.5 us -> 104 us (1.98)
  the two profiles are of different devices: /device:TPU:25 before, /device:TPU:0 now
where the time goes in v2:
time: 104 us; the launch traced here: 103 us
  Pallas kernels  102 us (98%)
  between operations  1.29 us (1%)
    pallas_call x1, Pallas kernels, on_device(): pl.pallas_call(store, out_shape=out_shape, in_specs=[hbm] * 5, out_specs=...  60.7 us
    pallas_call x1, Pallas kernels, on_device(): pl.pallas_call(functools.partial(kernel, dims), out_shape=out_shape, in_s...  41.5 us

profile of v2, /device:TPU:0, one launch (start us, length us, event | category | flops | bytes accessed | tf_op | source)
XLA Modules:
  0.0 103.4 jit_solution(10967007965326672709)
XLA Ops:
  1.3 41.5 %shard_map.128 = (bf16[256,256]{1,0:T(8,128)(2,1)}, f32[256,256]{1,0:T(8,128)}, f32[256,512]{1,0:T(8,128)}, f32[256,512]{1,0:T(8,128)}, f32[512,256]{1,0:T(8,128)}) custom-call(bf16[1024,256]{1,0:T(8,128)(2,1)} %state_hbm.1, s32[1,1024]{1,0:T(1,128)} %memb_hbm.1, f32[1,256]{1,0:T(1,128)} %bitcast.2, bf16[256,512]{1,0:T(8,128)(2,1)} %wr_hbm.1, ...), custom_call_target="tpu_custom_call" | custom-call | tf_op jit(solution)/shard_map/pallas_call | solution.py:512
  42.7 60.7 %shard_map.129 = (bf16[256,256]{1,0:T(8,128)(2,1)}, f32[256,256]{1,0:T(8,128)}, f32[256,512]{1,0:T(8,128)}, f32[256,512]{1,0:T(8,128)}, f32[512,256]{1,0:T(8,128)}) custom-call(bf16[256,256]{1,0:T(8,128)(2,1)} %get-tuple-element.10.new_in, f32[256,256]{1,0:T(8,128)} %get-tuple-element.11.gst_in, f32[256,512]{1,0:T(8,128)} %get-tuple-element.12.gr_in, ...), custom_call_target="tpu_custom_call" | custom-call | tf_op jit(solution)/shard_map/pallas_call | solution.py:580

commit v3 on v2

--- a/solution.py
+++ b/solution.py
@@ -9,7 +9,8 @@
 from jax.sharding import PartitionSpec as P
 
 BLK = 128
-CHUNK = 16
+CHUNK = 32
+LANES = 128
 BF16 = jnp.bfloat16
 F32 = jnp.float32
 MESH = pl.DeviceIdType.MESH
@@ -257,20 +258,22 @@
                 )
             )
     marks = jnp.concatenate(marks, axis=0)
-    mask[...] = dot(marks, jnp.ones((marks.shape[0], quarter), BF16), ((0,), (0,)))
-    proj[...] = dot(win[...].astype(BF16), ws) * BETA
-
-    def one_block(a):
+    mask[...] = dot(marks, jnp.ones((marks.shape[0], LANES), BF16), ((0,), (0,)))
+    passes = quarter // LANES
+    for p in range(passes):
+        proj[p, :, :] = dot(win[...].astype(BF16), ws_ref[:, p * LANES : (p + 1) * LANES]) * BETA
+
+    def one_block(a, p, cols):
         def one_chunk(c, carry):
             here = pl.ds(pl.multiple_of(a * BLK + c * CHUNK, CHUNK), CHUNK)
-            v0 = pre_buf[here, :]
-            da = dact_buf[here, :]
-            act_sum = jnp.zeros((CHUNK, quarter), F32)
-            d_sum = jnp.zeros((CHUNK, quarter), F32)
+            v0 = pre_buf[here, cols]
+            da = dact_buf[here, cols]
+            act_sum = jnp.zeros((CHUNK, LANES), F32)
+            d_sum = jnp.zeros((CHUNK, LANES), F32)
             for d in range(2 * blocks + 1):
                 if d == blocks:
                     continue
-                v = v0 + proj[pl.ds(a + d, 1), :]
+                v = v0 + proj[p, pl.ds(a + d, 1), :]
                 v2 = v * v
                 t = jnp.tanh(v * (v2 + KAPPA))
                 rise = (1.0 + t) * mask[pl.ds(a * span + d, 1), :]
@@ -283,41 +286,131 @@
                 total = d_pre[0:8, :]
                 for i in range(1, CHUNK // 8):
                     total = total + d_pre[i * 8 : (i + 1) * 8, :]
-                pg_buf[pg, :] = pg_buf[pg, :] + total
-            a_buf[here, :] = (act_sum * (0.5 / BETA)).astype(BF16)
-            d_buf[here, :] = (d_sum * 0.5).astype(BF16)
+                pg_buf[pg, cols] = pg_buf[pg, cols] + total
+            a_buf[here, cols] = (act_sum * (0.5 / BETA)).astype(BF16)
+            d_buf[here, cols] = (d_sum * 0.5).astype(BF16)
             return carry
 
         lax.fori_loop(0, BLK // CHUNK, one_chunk, 0)
 
+    travel = w_send.dtype
+    share = 3 * width // nz
+
+    def share_at(index):
+        return pl.ds(pl.multiple_of(index * share, share), share)
+
+    def start_reduce(p, cols):
+        pg = jnp.sum(pg_buf[:, cols].reshape(3 * blocks, 8, LANES), axis=1) * 0.5
+        w_loc[p, 0:width, :] = dot(x_buf[...], d_buf[:, cols], ((0,), (0,)))
+        w_loc[p, width : 2 * width, :] = dot(win[...], pg, ((0,), (0,)), HIGH)
+        outer = dot(a_buf[:, cols], cot_ref[...], ((0,), (0,)))
+        for c in range(width // LANES):
+            w_loc[p, 2 * width + c * LANES : 2 * width + (c + 1) * LANES, :] = outer[
+                :, c * LANES : (c + 1) * LANES
+            ]
+        w_send[p, :, :] = w_loc[p].astype(travel)
+        started = []
+        for k in range(1, nz):
+            to = lax.rem(r + k, nz)
+            started.append(
+                send(
+                    w_send.at[p, share_at(to)],
+                    w_recv.at[p, k - 1],
+                    red_ss.at[p, k - 1],
+                    red_rs.at[p, k - 1],
+                    {"space": to},
+                )
+            )
+        return started
+
+    def forward(p, k):
+        origin = share_at(lax.rem(r + nz - k, nz))
+        return [
+            send(
+                w_all.at[0, p, origin],
+                w_all.at[ds, p, origin],
+                fwd_ss.at[p, ds - 1, k],
+                fwd_rs.at[p, ds - 1, k],
+                {"sub": lax.rem(s + ds, ns)},
+            )
+            for ds in range(1, ns)
+        ]
+
+    def start_gather(p, started):
+        for copy in started:
+            copy.wait_recv()
+        total = w_loc[p, share_at(r), :]
+        for k in range(1, nz):
+            total = total + w_recv[p, k - 1].astype(F32)
+        w_all[0, p, share_at(r), :] = total.astype(travel)
+        gathered = [
+            send(
+                w_all.at[0, p, share_at(r)],
+                w_all.at[0, p, share_at(r)],
+                gat_ss.at[p, k - 1],
+                gat_rs.at[p, k - 1],
+                {"space": lax.rem(r + k, nz)},
+            )
+            for k in range(1, nz)
+        ]
+        return gathered, forward(p, 0)
+
+    def finish_gather(p, gathered):
+        passed = []
+        for k in range(1, nz):
+            gathered[k - 1].wait_recv()
+            passed += forward(p, k)
+        return passed
+
+    def write_out(p, ds):
+        begin = pl.multiple_of(lax.rem(s + ns - ds, ns) * quarter + p * LANES, LANES)
+        at = pl.ds(begin, LANES)
+        gr_ref[:, at] = w_all[ds, p, 0:width, :].astype(F32)
+        gs_ref[:, at] = w_all[ds, p, width : 2 * width, :].astype(F32)
+        for c in range(width // LANES):
+            rows_c = slice(2 * width + c * LANES, 2 * width + (c + 1) * LANES)
+            go_ref[at, c * LANES : (c + 1) * LANES] = w_all[ds, p, rows_c, :].astype(F32)
+
     msg_copies = []
-    for n, (dh, ds) in enumerate(offsets):
-        ph, ps = peer(dh, ds)
-        first = (ph * ns + ps) * own_blocks
-
-        def step(i, carry, first=first):
-            one_block(first + i)
-            return carry
-
-        lax.fori_loop(0, own_blocks, step, 0)
-        here = pl.ds(pl.multiple_of(first * BLK, BLK), piece)
-        message = dot(a_buf[here, :], wo)
-        grads = dot(d_buf[here, :], wr, ((1,), (1,)))
-        if n < owners - 1:
-            msg_send[n, 0:piece, :] = message.astype(BF16)
-            msg_send[n, piece : 2 * piece, :] = grads.astype(BF16)
-            msg_copies.append(
-                send(
-                    msg_send.at[n],
-                    msg_recv.at[n],
-                    msg_ss.at[n],
-                    msg_rs.at[n],
-                    {"hidden": ph, "sub": ps},
+    reduces = []
+    gathers = []
+    forwards = []
+    for p in range(passes):
+        cols = slice(p * LANES, (p + 1) * LANES)
+        for n, (dh, ds) in enumerate(offsets):
+            ph, ps = peer(dh, ds)
+            first = (ph * ns + ps) * own_blocks
+
+            def step(i, carry, first=first, p=p, cols=cols):
+                one_block(first + i, p, cols)
+                return carry
+
+            lax.fori_loop(0, own_blocks, step, 0)
+            if p > 0 and n == owners // 2:
+                gathered, passed = start_gather(p - 1, reduces[p - 1])
+                gathers.append(gathered)
+                forwards.append(passed)
+            if p < passes - 1:
+                continue
+            here = pl.ds(pl.multiple_of(first * BLK, BLK), piece)
+            message = dot(a_buf[here, :], wo)
+            grads = dot(d_buf[here, :], wr, ((1,), (1,)))
+            if n < owners - 1:
+                msg_send[n, 0:piece, :] = message.astype(BF16)
+                msg_send[n, piece : 2 * piece, :] = grads.astype(BF16)
+                msg_copies.append(
+                    send(
+                        msg_send.at[n],
+                        msg_recv.at[n],
+                        msg_ss.at[n],
+                        msg_rs.at[n],
+                        {"hidden": ph, "sub": ps},
+                    )
                 )
-            )
-        else:
-            own_msg[0:piece, :] = message
-            own_msg[piece : 2 * piece, :] = grads
+            else:
+                own_msg[0:piece, :] = message
+                own_msg[piece : 2 * piece, :] = grads
+        reduces.append(start_reduce(p, cols))
 
     pg = jnp.sum(pg_buf[...].reshape(3 * blocks, 8, quarter), axis=1) * 0.5
     sg_loc[...] = dot(pg, ws.astype(F32), ((1,), (1,)), HIGH)
@@ -331,32 +424,8 @@
         )
         for n, (other, place) in enumerate(((before, 0), (after, 2 * blocks)))
     ]
-
-    w_loc[0:width, :] = dot(x_buf[...], d_buf[...], ((0,), (0,)))
-    w_loc[width : 2 * width, :] = dot(win[...], pg, ((0,), (0,)), HIGH)
-    for c in range(width // quarter):
-        w_loc[2 * width + c * quarter : 2 * width + (c + 1) * quarter, :] = dot(
-            a_buf[...], cot_ref[:, c * quarter : (c + 1) * quarter], ((0,), (0,))
-        )
-    travel = w_send.dtype
-    w_send[...] = w_loc[...].astype(travel)
-    share = 3 * width // nz
-
-    def share_at(index):
-        return pl.ds(pl.multiple_of(index * share, share), share)
-
-    reduces = []
-    for k in range(1, nz):
-        to = lax.rem(r + k, nz)
-        reduces.append(
-            send(
-                w_send.at[share_at(to)],
-                w_recv.at[k - 1],
-                red_ss.at[k - 1],
-                red_rs.at[k - 1],
-                {"space": to},
-            )
-        )
+    for p in range(passes - 1):
+        forwards[p] += finish_gather(p, gathers[p])
 
     for copy in near:
         copy.wait()
@@ -373,40 +442,12 @@
                 {"hidden": ph, "sub": ps},
             )
         )
-
-    for copy in reduces:
-        copy.wait_recv()
-    total = w_loc[share_at(r), :]
-    for k in range(1, nz):
-        total = total + w_recv[k - 1].astype(F32)
-    w_all[0, share_at(r), :] = total.astype(travel)
-    gathers = []
-    forwards = []
-    for k in range(1, nz):
-        gathers.append(
-            send(
-                w_all.at[0, share_at(r)],
-                w_all.at[0, share_at(r)],
-                gat_ss.at[k - 1],
-                gat_rs.at[k - 1],
-                {"space": lax.rem(r + k, nz)},
-            )
-        )
-
-    def forward(k):
-        origin = share_at(lax.rem(r + nz - k, nz))
-        for ds in range(1, ns):
-            forwards.append(
-                send(
-                    w_all.at[0, origin],
-                    w_all.at[ds, origin],
-                    fwd_ss.at[ds - 1, k],
-                    fwd_rs.at[ds - 1, k],
-                    {"sub": lax.rem(s + ds, ns)},
-                )
-            )
-
-    forward(0)
+    for p in range(passes - 1):
+        write_out(p, 0)
+
+    gathered, passed = start_gather(passes - 1, reduces[passes - 1])
+    gathers.append(gathered)
+    forwards.append(passed)
 
     for copy in msg_copies:
         copy.wait()
@@ -438,41 +479,34 @@
         factor * scaled - xs * factor * factor * factor * inner + cot_ref[mine, :].astype(F32)
     )
 
-    for k in range(1, nz):
-        gathers[k - 1].wait_recv()
-        forward(k)
-    for copy in forwards:
+    for p in range(passes - 1):
+        for copy in forwards[p]:
+            copy.wait_recv()
+        for ds in range(1, ns):
+            write_out(p, ds)
+    last = passes - 1
+    forwards[last] += finish_gather(last, gathers[last])
+    write_out(last, 0)
+    for copy in forwards[last]:
         copy.wait_recv()
-    for ds in range(ns):
-        begin = pl.multiple_of(lax.rem(s + ns - ds, ns) * quarter, quarter)
-        cols = pl.ds(begin, quarter)
-        gr_ref[:, cols] = w_all[ds, 0:width, :].astype(F32)
-        gs_ref[:, cols] = w_all[ds, width : 2 * width, :].astype(F32)
-        for c in range(width // quarter):
-            at = 2 * width + c * quarter
-            go_ref[cols, c * quarter : (c + 1) * quarter] = w_all[ds, at : at + quarter, :].astype(
-                F32
-            )
-    for copy in reduces + gathers + forwards:
-        copy.wait_send()
-
-
-def store(new_in, gst_in, gr_in, gs_in, go_in, new_out, gst_out, gr_out, gs_out, go_out, sem):
-    copies = [
-        pltpu.make_async_copy(src, dst, sem.at[n])
-        for n, (src, dst) in enumerate(
-            (
-                (gr_in, gr_out),
-                (gs_in, gs_out),
-                (go_in, go_out),
-                (gst_in, gst_out),
-                (new_in, new_out),
-            )
-        )
-    ]
-    for copy in copies:
-        copy.start()
-    for copy in copies:
+    for ds in range(1, ns):
+        write_out(last, ds)
+    for p in range(passes):
+        for copy in reduces[p] + gathers[p] + forwards[p]:
+            copy.wait_send()
+
+
+def store(*refs):
+    ins, outs, held, (sem,) = refs[:5], refs[5:10], refs[10:15], refs[15:]
+    loads = [pltpu.make_async_copy(ins[n], held[n], sem.at[0, n]) for n in range(5)]
+    for load in loads:
+        load.start()
+    stores = []
+    for n in (0, 1, 2, 3, 4):
+        loads[n].wait()
+        stores.append(pltpu.make_async_copy(held[n], outs[n], sem.at[1, n]))
+        stores[-1].start()
+    for copy in stores:
         copy.wait()
 
 
@@ -496,6 +530,7 @@
     quarter = hid_dev // ns
     owners = nh * ns
     piece = rows // owners
+    passes = quarter // LANES
     share = 3 * width // nz
     travel = BF16 if share % 16 == 0 else F32
     dma = pltpu.SemaphoreType.DMA
@@ -527,8 +562,8 @@
             pltpu.VMEM((rows, width), BF16),
             pltpu.VMEM((2 * ns, 2 * slots, 128), jnp.int32),
             pltpu.VMEM((3 * blocks, width), F32),
-            pltpu.VMEM((3 * blocks, quarter), F32),
-            pltpu.VMEM((4 * blocks * blocks, quarter), F32),
+            pltpu.VMEM((passes, 3 * blocks, LANES), F32),
+            pltpu.VMEM((4 * blocks * blocks, LANES), F32),
             pltpu.VMEM((rows, quarter), F32),
             pltpu.VMEM((rows, quarter), F32),
             pltpu.VMEM((rows, quarter), BF16),
@@ -541,10 +576,10 @@
             pltpu.VMEM((2, blocks, width), F32),
             pltpu.VMEM((blocks, width), F32),
             pltpu.VMEM((owners - 1, blocks, width), F32),
-            pltpu.VMEM((3 * width, quarter), F32),
-            pltpu.VMEM((3 * width, quarter), travel),
-            pltpu.VMEM((nz - 1, share, quarter), travel),
-            pltpu.VMEM((ns, 3 * width, quarter), travel),
+            pltpu.VMEM((passes, 3 * width, LANES), F32),
+            pltpu.VMEM((passes, 3 * width, LANES), travel),
+            pltpu.VMEM((passes, nz - 1, share, LANES), travel),
+            pltpu.VMEM((ns, passes, 3 * width, LANES), travel),
             dma((8,)),
             dma((2 * ns - 1,)),
             dma((2 * ns - 1,)),
@@ -556,12 +591,12 @@
             dma((2,)),
             dma((owners - 1,)),
             dma((owners - 1,)),
-            dma((nz - 1,)),
-            dma((nz - 1,)),
-            dma((nz - 1,)),
-            dma((nz - 1,)),
-            dma((ns - 1, nz)),
-            dma((ns - 1, nz)),
+            dma((passes, nz - 1)),
+            dma((passes, nz - 1)),
+            dma((passes, nz - 1)),
+            dma((passes, nz - 1)),
+            dma((passes, ns - 1, nz)),
+            dma((passes, ns - 1, nz)),
         ],
         compiler_params=pltpu.CompilerParams(
             collective_id=0, has_side_effects=True, vmem_limit_bytes=64 * 1024 * 1024
@@ -582,7 +617,7 @@
         out_shape=out_shape,
         in_specs=[hbm] * 5,
         out_specs=(hbm,) * 5,
-        scratch_shapes=[dma((5,))],
+        scratch_shapes=[pltpu.VMEM(one.shape, one.dtype) for one in out_shape] + [dma((2, 5))],
         compiler_params=pltpu.CompilerParams(vmem_limit_bytes=64 * 1024 * 1024),
     )(*results)
 

time: 104 us -> 42.9 us (0.41)
  Pallas kernels: 102 us -> 41.4 us
    pallas_call x1, Pallas kernels: 60.7 us -> 2.42 us  [on_device(): pl.pallas_call(store, out_shape=out_shape, in_specs=[hbm] * 5, out_specs=...]
    pallas_call x1, Pallas kernels: 41.5 us -> 38.9 us  [on_device(): pl.pallas_call(functools.partial(kernel, dims), out_shape=out_shape, in_s...]
where the time goes in v3:
time: 42.9 us; the launch traced here: 42.7 us
  Pallas kernels  41.4 us (97%)
  between operations  1.29 us (3%)
    pallas_call x1, Pallas kernels, on_device(): pl.pallas_call(functools.partial(kernel, dims), out_shape=out_shape, in_s...  38.9 us
    pallas_call x1, Pallas kernels, on_device(): pl.pallas_call(store, out_shape=out_shape, in_specs=[hbm] * 5, out_specs=...  2.42 us

profile of v3, /device:TPU:0, one launch (start us, length us, event | category | flops | bytes accessed | tf_op | source)
XLA Modules:
  0.0 42.7 jit_solution(17309977778385967102)
XLA Ops:
  1.3 38.9 %shard_map.128 = (bf16[256,256]{1,0:T(8,128)(2,1)}, f32[256,256]{1,0:T(8,128)}, f32[256,512]{1,0:T(8,128)}, f32[256,512]{1,0:T(8,128)}, f32[512,256]{1,0:T(8,128)}) custom-call(bf16[1024,256]{1,0:T(8,128)(2,1)} %state_hbm.1, s32[1,1024]{1,0:T(1,128)} %memb_hbm.1, f32[1,256]{1,0:T(1,128)} %bitcast.2, bf16[256,512]{1,0:T(8,128)(2,1)} %wr_hbm.1, ...), custom_call_target="tpu_custom_call" | custom-call | tf_op jit(solution)/shard_map/pallas_call | solution.py:547
  40.2 2.4 %shard_map.129 = (bf16[256,256]{1,0:T(8,128)(2,1)}, f32[256,256]{1,0:T(8,128)}, f32[256,512]{1,0:T(8,128)}, f32[256,512]{1,0:T(8,128)}, f32[512,256]{1,0:T(8,128)}) custom-call(bf16[256,256]{1,0:T(8,128)(2,1)} %get-tuple-element.10.refs_0_, f32[256,256]{1,0:T(8,128)} %get-tuple-element.11.refs_1_, f32[256,512]{1,0:T(8,128)} %get-tuple-element.12.refs_2_, ...), custom_call_target="tpu_custom_call" | custom-call | tf_op jit(solution)/shard_map/pallas_call | solution.py:615
